TPU v7x, 32 devices: a whole 2x2x4 slice. The times are simulated.
32 devices in a mesh: grp: 2 (over x), ra: 16 (over z, y, core).
Axes of the slice: x: 2, y: 2, z: 4, core: 2. Of those that a mesh axis runs over, the one named last changes fastest.
Arguments:
- observed_correlations: bfloat16 [1536, 351, 128], P(('grp', 'ra')), parts along dimension 0
- direction_per_batch: int32 [1536, 1], P(('grp', 'ra')), parts along dimension 0, may hold values from 0 to 15; in each aligned block of 48 rows (0 to 47, 48 to 95, ...) at most 6 rows name the same one
- receiver_pairings: int32 [702, 2], P('grp'), parts along dimension 0, may hold values from 0 to 26, as said below
- predicted_source_brightness: float32 [32, 16], P(('grp', 'ra')), parts along dimension 0, may hold values from 0.5 to 2
- starter_complex_factors: float32 [32, 2, 27, 16], P(('grp', 'ra')), parts along dimension 0, may hold values from 0.5 to 1.5
Outputs:
- solved_gains: float32 [32, 2, 27, 16], P(('grp', 'ra')), parts along dimension 0
There are 2 independent parts, one for each index of `grp`. A program takes and returns all parts, laid end to end along the dimension named above; each array names one. Nothing has to cross between parts.
Inputs may be any that keep to these rules, and one draw needn't show every extreme that they name: `direction_per_batch`: among the 48 blocks held by one device, at most 6 name the same pointing. `receiver_pairings`: every unordered pair of two different antennas stands in exactly one row, in either order.
All inputs are finite; a program needn't handle non-finite values.
Results may differ from a plain program's by a relative error of at most 0.0003.
Values may be sent and summed in bfloat16 or wider, within the bound.
A program may use at most 128 MiB of HBM per device.

v0:
```python
import math

import jax
import jax.numpy as jnp
from jax import lax
from jax.sharding import PartitionSpec as P

ANTENNA_COUNT = 27
SPW = 16
ITERS = 2


ROBUST = 0.5
COUPLING = 0.2
DAMPING = 100.0
PRECISE = lax.Precision.HIGHEST


def with_halo(cells, sides, width):
    for axis, dim in sides:
        count = lax.axis_size(axis)
        head = lax.slice_in_dim(cells, 0, width, axis=dim)
        tail = lax.slice_in_dim(cells, cells.shape[dim] - width, cells.shape[dim], axis=dim)
        cells = jnp.concatenate(
            [
                lax.ppermute(tail, axis, [(i, (i + 1) % count) for i in range(count)]),
                cells,
                lax.ppermute(head, axis, [((i + 1) % count, i) for i in range(count)]),
            ],
            axis=dim,
        )
    return cells


def channel_sums(operands):
    blocks_data, pred_re, pred_im = operands
    middle = blocks_data.shape[-1] // 2
    data = blocks_data.astype(jnp.float32)
    data_re = data[..., :middle]
    data_im = data[..., middle:]
    resid_re = data_re - pred_re[..., None]
    resid_im = data_im - pred_im[..., None]
    weight = 1.0 / (1.0 + (resid_re * resid_re + resid_im * resid_im) / ROBUST)
    return (
        jnp.sum(weight, axis=-1),
        jnp.sum(weight * data_re, axis=-1),
        jnp.sum(weight * data_im, axis=-1),
    )


def grouped_sums(
    blocks_data, leading_real, leading_imaginary, trailing_real, trailing_imaginary, flux_rows
):
    pred_re = flux_rows[:, None] * (
        leading_real * trailing_real + leading_imaginary * trailing_imaginary
    )
    pred_im = flux_rows[:, None] * (
        leading_imaginary * trailing_real - leading_real * trailing_imaginary
    )
    row_count = blocks_data.shape[0]
    group_size = math.gcd(row_count, 32)
    groups = row_count // group_size
    shaped = blocks_data.reshape((groups, group_size) + blocks_data.shape[1:])
    totals = lax.map(
        channel_sums,
        (shaped, pred_re.reshape(groups, group_size, -1), pred_im.reshape(groups, group_size, -1)),
    )
    return tuple((member.reshape(row_count, -1) for member in totals))


def normal_terms(
    leading_real, leading_imaginary, trailing_real, trailing_imaginary, flux_rows, totals
):
    weight_sum, weighted_re, weighted_im = totals
    scale = flux_rows[:, None]
    to_first = (
        scale * (trailing_real * weighted_re - trailing_imaginary * weighted_im),
        scale * (trailing_real * weighted_im + trailing_imaginary * weighted_re),
        scale
        * scale
        * (trailing_real * trailing_real + trailing_imaginary * trailing_imaginary)
        * weight_sum,
    )
    to_second = (
        scale * (leading_real * weighted_re + leading_imaginary * weighted_im),
        scale * (leading_imaginary * weighted_re - leading_real * weighted_im),
        scale
        * scale
        * (leading_real * leading_real + leading_imaginary * leading_imaginary)
        * weight_sum,
    )
    return (to_first, to_second)


def antenna_normals(
    to_first, to_second, first_receiver_indicator, second_receiver_indicator, row_hot
):
    results = []
    for one_first, one_second in zip(to_first, to_second):
        per_row = jnp.dot(one_first, first_receiver_indicator, precision=PRECISE) + jnp.dot(
            one_second, second_receiver_indicator, precision=PRECISE
        )
        results.append(jnp.dot(row_hot.T, per_row, precision=PRECISE))
    return jnp.stack(results, axis=0)


def advance(normals, current, preceding, following):
    numer_re = normals[0].T
    numer_im = normals[1].T
    denom = normals[2].T
    own_re = (numer_re + DAMPING * current[0]) / (denom + DAMPING)
    own_im = (numer_im + DAMPING * current[1]) / (denom + DAMPING)
    own = jnp.stack([own_re, own_im], axis=0)
    return (1.0 - 2.0 * COUPLING) * own + COUPLING * (preceding + following)


def body(
    observed_correlations,
    direction_per_batch,
    receiver_pairings,
    predicted_source_brightness,
    starter_complex_factors,
):
    held_blocks = observed_correlations.shape[0]
    receiver_roster = jnp.arange(ANTENNA_COUNT, dtype=jnp.int32)
    first_receiver_indicator = (receiver_pairings[:, 0:1] == receiver_roster[None, :]).astype(
        jnp.float32
    )
    second_receiver_indicator = (receiver_pairings[:, 1:2] == receiver_roster[None, :]).astype(
        jnp.float32
    )
    windows = jnp.arange(SPW, dtype=jnp.int32)
    window_of = jnp.arange(held_blocks, dtype=jnp.int32) % SPW
    target = direction_per_batch[:, 0]
    devices = lax.axis_size("ra")
    current = starter_complex_factors[0]
    capacity = max(2, 2 * held_blocks // devices)
    positions = jnp.arange(held_blocks, dtype=jnp.int32)
    earlier_same = (target[:, None] == target[None, :]) & (positions[None, :] < positions[:, None])
    position_rank = jnp.sum(earlier_same.astype(jnp.int32), axis=1)
    slot_of = target * capacity + position_rank
    slot_index = jnp.arange(devices * capacity, dtype=jnp.int32)
    matches = (slot_index[:, None] == slot_of[None, :]).astype(jnp.int32)
    occupied = jnp.sum(matches, axis=1)
    source_row = jnp.sum(matches * positions[None, :], axis=1)
    outgoing = jnp.where(
        occupied[:, None, None] > 0,
        observed_correlations[source_row],
        jnp.zeros((), observed_correlations.dtype),
    )
    labels = jnp.stack([window_of[source_row], occupied], axis=1)
    arrived, arrived_labels = (
        lax.all_to_all(outgoing, "ra", split_axis=0, concat_axis=0, tiled=True),
        lax.all_to_all(labels, "ra", split_axis=0, concat_axis=0, tiled=True),
    )
    band_hot = (arrived_labels[:, 0:1] == windows[None, :]).astype(jnp.float32) * arrived_labels[
        :, 1:2
    ].astype(jnp.float32)
    flux_rows = jnp.dot(band_hot, predicted_source_brightness[0], precision=PRECISE)
    for iteration in range(ITERS):
        leading_real = jnp.dot(
            band_hot,
            jnp.dot(first_receiver_indicator, current[0], precision=PRECISE).T,
            precision=PRECISE,
        )
        leading_imaginary = jnp.dot(
            band_hot,
            jnp.dot(first_receiver_indicator, current[1], precision=PRECISE).T,
            precision=PRECISE,
        )
        trailing_real = jnp.dot(
            band_hot,
            jnp.dot(second_receiver_indicator, current[0], precision=PRECISE).T,
            precision=PRECISE,
        )
        trailing_imaginary = jnp.dot(
            band_hot,
            jnp.dot(second_receiver_indicator, current[1], precision=PRECISE).T,
            precision=PRECISE,
        )
        totals = grouped_sums(
            arrived, leading_real, leading_imaginary, trailing_real, trailing_imaginary, flux_rows
        )
        to_first, to_second = normal_terms(
            leading_real, leading_imaginary, trailing_real, trailing_imaginary, flux_rows, totals
        )
        normals = antenna_normals(
            to_first, to_second, first_receiver_indicator, second_receiver_indicator, band_hot
        )
        neighbours = with_halo(current[None], (("ra", 0),), 1)
        current = advance(normals, current, neighbours[0], neighbours[2])
    return current[None]


def solution(mesh):
    placed = (
        P(("grp", "ra"), None, None),
        P(("grp", "ra"), None),
        P("grp", None),
        P(("grp", "ra"), None),
        P(("grp", "ra"), None, None, None),
    )
    return jax.shard_map(
        body,
        mesh=mesh,
        in_specs=placed,
        out_specs=P(("grp", "ra"), None, None, None),
        check_vma=False,
    )
```

profile of v0, /device:TPU:0, one launch (start us, length us, event | category | flops | bytes accessed | tf_op | source)
XLA Modules:
  0.0 353.5 jit_solution(5284404443804486196)
XLA Ops:
  0.0 0.9 convert_reduce_fusion.1
  0.9 0.7 multiply_add_fusion
  1.8 1.2 gather_fusion
  3.1 0.6 copy.14
  3.7 7.4 %all-to-all-start = ((s32[16,6,2]{1,2,0:T(2,128)}), s32[16,6,2]{1,2,0:T(2,128)S(1)}, u32[]{:S(2)}, u32[]{:S(2)}) async-start(s32[16,6,2]{1,2,0:T(2,128)} %copy.14), calls=%async_computation | async-start | bytes 32768 | tf_op jit(solution)/shard_map/all_to_all | solution.py:154
  11.1 39.3 %gather_fusion.1 = bf16[96,351,128]{2,0,1:T(8,128)(2,1)} fusion(bf16[48,351,128]{2,0,1:T(8,128)(2,1)} %param.9, s32[1024]{0:T(1024)S(1)} %pad_clamp_fusion), kind=kCustom, calls=%fused_computation.1 | custom fusion | bytes 17252736 | tf_op jit(solution)/shard_map/gather | solution.py:148
  50.5 7.4 %broadcast_select_fusion = bf16[96,351,128]{2,0,1:T(8,128)(2,1)} fusion(bf16[96,351,128]{2,0,1:T(8,128)(2,1)} %gather_fusion.1, pred[96]{0:T(512)(128)(4,1)S(1)} %broadcast_compare_fusion), kind=kLoop, calls=%fused_computation.20 | loop fusion | flops 4313088 | bytes 17252448 | tf_op jit(solution)/shard_map/jit(_where)/select_n | solution.py:146
  57.8 10.1 %copy.16 = bf16[96,351,128]{2,1,0:T(8,128)(2,1)} copy(bf16[96,351,128]{2,0,1:T(8,128)(2,1)} %broadcast_select_fusion) | data formatting | bytes 17252352 | tf_op jit(solution)/shard_map/jit(_where)/select_n | solution.py:146
  67.9 6.2 %all-to-all-start.1 = ((bf16[96,351,128]{2,1,0:T(8,128)(2,1)}), bf16[96,351,128]{2,1,0:T(8,128)(2,1)}, u32[]{:S(2)}, u32[]{:S(2)}) async-start(bf16[96,351,128]{2,1,0:T(8,128)(2,1)} %copy.16), calls=%async_computation.1 | async-start | bytes 17301504 | tf_op jit(solution)/shard_map/all_to_all | solution.py:153
  74.1 0.4 collective-permute-start
  74.6 4.1 %collective-permute-start.1 = (f32[1,2,27,16]{2,3,1,0:T(8,128)S(1)}, f32[1,2,27,16]{2,3,1,0:T(8,128)S(1)}, u32[]{:S(2)}, u32[]{:S(2)}) collective-permute-start(f32[1,2,27,16]{2,3,1,0:T(8,128)S(1)} %copy-done.2), channel_id=1, source_target_pairs={{1,0},{2,1},{3,2},{4,3},{5,4},{6,5},{7,6},{8,7},{9,8},{10,9},{11,1... | collective-permute-start | bytes 10376 | tf_op jit(solution)/shard_map/ppermute | solution.py:28
  78.7 0.3 fusion.41
  78.9 0.3 fusion.42
  79.2 0.3 fusion.37
  79.5 0.3 fusion.38
  80.0 0.2 fusion.153
  80.2 0.4 fusion.22
  80.6 0.3 fusion.20
  80.9 0.3 fusion.26
  81.2 0.3 subtract_multiply_fusion.1
  81.6 148.0 %all-to-all-done.1 = bf16[96,351,128]{2,1,0:T(8,128)(2,1)} async-done(((bf16[96,351,128]{2,1,0:T(8,128)(2,1)}), bf16[96,351,128]{2,1,0:T(8,128)(2,1)}, u32[]{:S(2)}, u32[]{:S(2)}) %all-to-all-start.1) | async-done | bytes 8626208 | tf_op jit(solution)/shard_map/all_to_all | solution.py:153
  229.6 38.6 %while.28 = (s32[]{:T(128)}, f32[3,32,351]{2,1,0:T(8,128)S(1)}, f32[3,32,351]{2,1,0:T(8,128)S(1)}, f32[3,32,351]{2,1,0:T(8,128)S(1)}, bf16[3,32,351,128]{3,2,1,0...) while((s32[]{:T(128)}, f32[3,32,351]{2,1,0:T(8,128)S(1)}, ...), condition=%wide.region_7.8_spmd, body=%wide.region_3.7_spmd.sunk | while | flops 10749026 | bytes 15076337 | solution.py:64
  229.7 2.5 bitcast_convert_fusion.4
  232.2 10.3 %multiply_reduce_fusion.6 = (f32[32,351]{1,0:T(8,128)S(1)}, f32[32,351]{1,0:T(8,128)S(1)}, f32[32,351]{1,0:T(8,128)S(1)}) fusion(f32[32,351,128]{2,1,0:T(8,128)S(1)} %bitcast_convert_fusion.4, f32[32,351]{1,0:T(8,128)S(1)} %dynamic-slice_bitcast_fusion.8, f32[32,351]{1,0:T(8,128)S(1)} %dynamic-slice_bitcast_fusion.9), kind=kLoop, calls=%fused_computation.2.clone.1 | loop fusion | flops 9311328 | bytes 5975424 | tf_op jit(solution)/shard_map/while/body/eval_jaxpr/reduce_sum | solution.py:47
  242.5 2.5 bitcast_convert_fusion.4
  245.1 10.3 %multiply_reduce_fusion.6 = (f32[32,351]{1,0:T(8,128)S(1)}, f32[32,351]{1,0:T(8,128)S(1)}, f32[32,351]{1,0:T(8,128)S(1)}) fusion(f32[32,351,128]{2,1,0:T(8,128)S(1)} %bitcast_convert_fusion.4, f32[32,351]{1,0:T(8,128)S(1)} %dynamic-slice_bitcast_fusion.8, f32[32,351]{1,0:T(8,128)S(1)} %dynamic-slice_bitcast_fusion.9), kind=kLoop, calls=%fused_computation.2.clone.1 | loop fusion | flops 9311328 | bytes 5975424 | tf_op jit(solution)/shard_map/while/body/eval_jaxpr/reduce_sum | solution.py:47
  255.4 2.5 bitcast_convert_fusion.4
  257.9 10.3 %multiply_reduce_fusion.6 = (f32[32,351]{1,0:T(8,128)S(1)}, f32[32,351]{1,0:T(8,128)S(1)}, f32[32,351]{1,0:T(8,128)S(1)}) fusion(f32[32,351,128]{2,1,0:T(8,128)S(1)} %bitcast_convert_fusion.4, f32[32,351]{1,0:T(8,128)S(1)} %dynamic-slice_bitcast_fusion.8, f32[32,351]{1,0:T(8,128)S(1)} %dynamic-slice_bitcast_fusion.9), kind=kLoop, calls=%fused_computation.2.clone.1 | loop fusion | flops 9311328 | bytes 5975424 | tf_op jit(solution)/shard_map/while/body/eval_jaxpr/reduce_sum | solution.py:47
  268.4 0.4 fusion.35
  268.8 0.4 convolution_add_fusion.4
  269.2 0.3 convolution_add_fusion.10
  269.5 0.4 fusion.34
  269.9 0.4 fusion.36
  270.3 0.4 convolution_add_fusion.3
  270.7 0.3 fusion.4
  271.0 0.4 convolution_add_fusion.5
  271.4 0.3 fusion.5
  271.8 0.3 fusion.32
  272.1 0.3 fusion.39
  272.4 0.3 fusion.40
  272.6 0.3 fusion.33
  273.0 0.8 collective-permute-start.2
  273.8 35.4 %collective-permute-start.3 = (f32[1,2,27,16]{2,3,1,0:T(8,128)S(1)}, f32[1,2,27,16]{2,3,1,0:T(8,128)S(1)}, u32[]{:S(2)}, u32[]{:S(2)}) collective-permute-start(f32[1,2,27,16]{2,3,1,0:T(8,128)S(1)} %fusion.127), channel_id=1, source_target_pairs={{1,0},{2,1},{3,2},{4,3},{5,4},{6,5},{7,6},{8,7},{9,8},{10,9},{11,1... | collective-permute-start | bytes 10376 | tf_op jit(solution)/shard_map/ppermute | solution.py:28
  309.2 0.3 fusion.11
  309.5 0.3 fusion.9
  309.8 0.3 fusion.15
  310.1 0.3 subtract_multiply_fusion
  310.6 38.8 %while.29 = (s32[]{:T(128)}, f32[3,32,351]{2,1,0:T(8,128)S(1)}, f32[3,32,351]{2,1,0:T(8,128)S(1)}, f32[3,32,351]{2,1,0:T(8,128)S(1)}, bf16[3,32,351,128]{3,2,1,0...) while((s32[]{:T(128)}, f32[3,32,351]{2,1,0:T(8,128)S(1)}, ...), condition=%wide.region_12.13_spmd, body=%wide.region_8.12_spmd.sunk | while | flops 10749026 | bytes 15076337 | solution.py:64
  310.8 2.5 bitcast_convert_fusion.5
  313.3 10.3 %multiply_reduce_fusion.7 = (f32[32,351]{1,0:T(8,128)S(1)}, f32[32,351]{1,0:T(8,128)S(1)}, f32[32,351]{1,0:T(8,128)S(1)}) fusion(f32[32,351,128]{2,1,0:T(8,128)S(1)} %bitcast_convert_fusion.5, f32[32,351]{1,0:T(8,128)S(1)} %dynamic-slice_bitcast_fusion.10, f32[32,351]{1,0:T(8,128)S(1)} %dynamic-slice_bitcast_fusion.11), kind=kLoop, calls=%fused_computation.11.clone.1 | loop fusion | flops 9311328 | bytes 5975424 | tf_op jit(solution)/shard_map/while/body/eval_jaxpr/reduce_sum | solution.py:47
  323.7 2.5 bitcast_convert_fusion.5
  326.2 10.3 %multiply_reduce_fusion.7 = (f32[32,351]{1,0:T(8,128)S(1)}, f32[32,351]{1,0:T(8,128)S(1)}, f32[32,351]{1,0:T(8,128)S(1)}) fusion(f32[32,351,128]{2,1,0:T(8,128)S(1)} %bitcast_convert_fusion.5, f32[32,351]{1,0:T(8,128)S(1)} %dynamic-slice_bitcast_fusion.10, f32[32,351]{1,0:T(8,128)S(1)} %dynamic-slice_bitcast_fusion.11), kind=kLoop, calls=%fused_computation.11.clone.1 | loop fusion | flops 9311328 | bytes 5975424 | tf_op jit(solution)/shard_map/while/body/eval_jaxpr/reduce_sum | solution.py:47
  336.5 2.5 bitcast_convert_fusion.5
  339.1 10.3 %multiply_reduce_fusion.7 = (f32[32,351]{1,0:T(8,128)S(1)}, f32[32,351]{1,0:T(8,128)S(1)}, f32[32,351]{1,0:T(8,128)S(1)}) fusion(f32[32,351,128]{2,1,0:T(8,128)S(1)} %bitcast_convert_fusion.5, f32[32,351]{1,0:T(8,128)S(1)} %dynamic-slice_bitcast_fusion.10, f32[32,351]{1,0:T(8,128)S(1)} %dynamic-slice_bitcast_fusion.11), kind=kLoop, calls=%fused_computation.11.clone.1 | loop fusion | flops 9311328 | bytes 5975424 | tf_op jit(solution)/shard_map/while/body/eval_jaxpr/reduce_sum | solution.py:47
  349.6 0.4 fusion.30
  349.9 0.4 convolution_add_fusion.1
  350.3 0.3 convolution_add_fusion.7
  350.6 0.4 fusion.29
  351.0 0.4 fusion.31
  351.4 0.4 convolution_add_fusion
  351.8 0.3 fusion.1
  352.1 0.4 convolution_add_fusion.2
  352.5 0.3 fusion.3
  352.9 0.6 fusion.126
  (57 shorter events, 1.2 us)
Async XLA Ops:
  0.0 80.0 %copy-start = (f32[1,16]{1,0:T(1,128)S(1)}, f32[1,16]{1,0:T(1,128)}, u32[]{:S(2)}) copy-start(f32[1,16]{1,0:T(1,128)} %param.12) | copy-start | bytes 196
  3.7 64.2 %all-to-all-start = ((s32[16,6,2]{1,2,0:T(2,128)}), s32[16,6,2]{1,2,0:T(2,128)S(1)}, u32[]{:S(2)}, u32[]{:S(2)}) async-start(s32[16,6,2]{1,2,0:T(2,128)} %copy.14), calls=%async_computation | async-start | bytes 32768 | tf_op jit(solution)/shard_map/all_to_all | solution.py:154
  67.9 6.2 %copy-start.2 = (f32[1,2,27,16]{2,3,1,0:T(8,128)S(1)}, f32[1,2,27,16]{2,3,1,0:T(8,128)}, u32[]{:S(2)}) copy-start(f32[1,2,27,16]{2,3,1,0:T(8,128)} %param.13) | copy-start | bytes 10372
  67.9 10.7 %copy-start.1 = (s32[351,2]{0,1:T(2,128)S(1)}, s32[351,2]{0,1:T(2,128)}, u32[]{:S(2)}) copy-start(s32[351,2]{0,1:T(2,128)} %param.11) | copy-start | bytes 8428
  67.9 161.6 %all-to-all-start.1 = ((bf16[96,351,128]{2,1,0:T(8,128)(2,1)}), bf16[96,351,128]{2,1,0:T(8,128)(2,1)}, u32[]{:S(2)}, u32[]{:S(2)}) async-start(bf16[96,351,128]{2,1,0:T(8,128)(2,1)} %copy.16), calls=%async_computation.1 | async-start | bytes 17301504 | tf_op jit(solution)/shard_map/all_to_all | solution.py:153
  74.1 197.6 %collective-permute-start = (f32[1,2,27,16]{2,3,1,0:T(8,128)S(1)}, f32[1,2,27,16]{2,3,1,0:T(8,128)S(1)}, u32[]{:S(2)}, u32[]{:S(2)}) collective-permute-start(f32[1,2,27,16]{2,3,1,0:T(8,128)S(1)} %copy-done.2), channel_id=1, source_target_pairs={{0,1},{1,2},{2,3},{3,4},{4,5},{5,6},{6,7},{7,8},{8,9},{9,10},{10,1... | collective-permute-start | bytes 10376 | tf_op jit(solution)/shard_map/ppermute | solution.py:26
  74.6 197.2 %collective-permute-start.1 = (f32[1,2,27,16]{2,3,1,0:T(8,128)S(1)}, f32[1,2,27,16]{2,3,1,0:T(8,128)S(1)}, u32[]{:S(2)}, u32[]{:S(2)}) collective-permute-start(f32[1,2,27,16]{2,3,1,0:T(8,128)S(1)} %copy-done.2), channel_id=1, source_target_pairs={{1,0},{2,1},{3,2},{4,3},{5,4},{6,5},{7,6},{8,7},{9,8},{10,9},{11,1... | collective-permute-start | bytes 10376 | tf_op jit(solution)/shard_map/ppermute | solution.py:28
  273.0 79.9 %collective-permute-start.2 = (f32[1,2,27,16]{2,3,1,0:T(8,128)S(1)}, f32[1,2,27,16]{2,3,1,0:T(8,128)S(1)}, u32[]{:S(2)}, u32[]{:S(2)}) collective-permute-start(f32[1,2,27,16]{2,3,1,0:T(8,128)S(1)} %fusion.127), channel_id=1, source_target_pairs={{0,1},{1,2},{2,3},{3,4},{4,5},{5,6},{6,7},{7,8},{8,9},{9,10},{10,1... | collective-permute-start | bytes 10376 | tf_op jit(solution)/shard_map/ppermute | solution.py:26
  273.8 79.1 %collective-permute-start.3 = (f32[1,2,27,16]{2,3,1,0:T(8,128)S(1)}, f32[1,2,27,16]{2,3,1,0:T(8,128)S(1)}, u32[]{:S(2)}, u32[]{:S(2)}) collective-permute-start(f32[1,2,27,16]{2,3,1,0:T(8,128)S(1)} %fusion.127), channel_id=1, source_target_pairs={{1,0},{2,1},{3,2},{4,3},{5,4},{6,5},{7,6},{8,7},{9,8},{10,9},{11,1... | collective-permute-start | bytes 10376 | tf_op jit(solution)/shard_map/ppermute | solution.py:28
where the time goes:
time: 354 us
  waiting for transfers between devices  148 us (42%)
  other arithmetic  86.6 us (24%)
  starting transfers between devices  54.2 us (15%)
  local copies, waits for them, and re-layouts  51.9 us (15%)
  matrix products  11.7 us (3%)
    all_to_all x1, waiting for transfers between devices, body(): lax.all_to_all(outgoing, 'ra', split_axis=0, concat_axis=0, tiled=True)  148 us
    reduce_sum x6, other arithmetic, channel_sums(): jnp.sum(weight * data_im, axis=-1)  61.6 us
    ppermute x2, starting transfers between devices, with_halo(): lax.ppermute(head, axis, [((i + 1) % count, i) for i in range(count)])  39.4 us
    gather x1, local copies, waits for them, and re-layouts, body(): observed_correlations[source_row]  39.3 us
    convert_element_type x6, other arithmetic, channel_sums(): data = blocks_data.astype(jnp.float32)  14.9 us
    select_n x1, local copies, waits for them, and re-layouts, body(): jnp.where(occupied[:, None, None] > 0, observed_correlations[source_row],...  10.1 us
    all_to_all x1, starting transfers between devices, body(): lax.all_to_all(labels, 'ra', split_axis=0, concat_axis=0, tiled=True)  7.39 us
    select_n x1, other arithmetic, body(): jnp.where(occupied[:, None, None] > 0, observed_correlations[source_row],...  7.37 us
  transfers between devices with their start and end apart: 6, of which 1 were waited for; matrix products, arithmetic and copies ran while one was open for 41% of the time, Pallas kernels for 0%

commit v1 on v0

v1 whole, which is shorter than its diff:
```python
import functools

import jax
import jax.numpy as jnp
from jax import lax
from jax.experimental import pallas as pl
from jax.experimental.pallas import tpu as pltpu
from jax.sharding import PartitionSpec as P

ITERS = 2
ROBUST = 0.5
COUPLING = 0.2
DAMPING = 100.0
PRECISE = lax.Precision.HIGHEST
F32 = jnp.float32
BF16 = jnp.bfloat16

GROUP = 8
PART = 32
LANES = 128
PIECE = 32


def dot(a, b, ca=1, cb=0):
    return lax.dot_general(
        a, b, (((ca,), (cb,)), ((), ())), precision=PRECISE, preferred_element_type=F32
    )


def iota(shape, dim):
    return lax.broadcasted_iota(jnp.int32, shape, dim)


def kernel(
    n,
    x_ref,
    target_ref,
    pair_ref,
    flux_ref,
    start_ref,
    out_ref,
    raw,
    turned,
    tables,
    mine,
    slabs,
    partials,
    pred,
    sums,
    hot_rows,
    hot_cols,
    x_sem,
    send_sem,
    recv_sem,
):
    base, held, width = x_ref.shape
    rows = raw.shape[0]
    chunks = rows // GROUP
    lanes = GROUP * held
    half = width // 2
    antennas = start_ref.shape[3]
    windows = start_ref.shape[2]
    me = lax.axis_index("ra")

    loads = []
    for k, low in enumerate(range(0, base, PIECE)):
        size = min(PIECE, base - low)
        copy = pltpu.make_async_copy(
            x_ref.at[pl.ds(low, size)], raw.at[pl.ds(low, size)], x_sem.at[k]
        )
        copy.start()
        loads.append(copy)

    barrier = pltpu.get_barrier_semaphore()

    def greet(k, carry):
        pl.semaphore_signal(
            barrier,
            inc=1,
            device_id={"ra": lax.rem(me + k, n)},
            device_id_type=pl.DeviceIdType.MESH,
        )
        return carry

    lax.fori_loop(1, n, greet, 0)

    eye = iota((windows, windows), 0) == iota((windows, windows), 1)
    flux_col = jnp.sum(jnp.where(eye, flux_ref[...], 0.0), axis=1, keepdims=True)
    mine[...] = jnp.zeros_like(mine)
    mine[0, :, 0:antennas] = start_ref[0, 0]
    mine[0, :, PART : PART + antennas] = start_ref[0, 1]
    mine[0, :, 2 * PART : 2 * PART + 1] = flux_col

    pl.semaphore_wait(barrier, n - 1)

    def copy_to(phase, source, place, k):
        return pltpu.make_async_remote_copy(
            src_ref=source,
            dst_ref=place.at[me],
            send_sem=send_sem.at[phase],
            recv_sem=recv_sem.at[phase],
            device_id={"ra": lax.rem(me + k, n)},
            device_id_type=pl.DeviceIdType.MESH,
        )

    def send_gains(phase, it):
        def step(k, carry):
            copy_to(phase, mine.at[it], tables.at[it], k).start()
            return carry

        lax.fori_loop(1, n, step, 0)
        tables[it, me] = mine[it]

    def send_slabs(phase, it):
        def step(k, carry):
            copy_to(phase, slabs.at[it, lax.rem(me + k, n)], partials.at[it], k).start()
            return carry

        lax.fori_loop(1, n, step, 0)
        partials[it, me] = slabs[it, me]

    def finish(phase, place):
        whole = place.at[pl.ds(0, n - 1)]
        both = pltpu.make_async_remote_copy(
            src_ref=whole,
            dst_ref=whole,
            send_sem=send_sem.at[phase],
            recv_sem=recv_sem.at[phase],
            device_id={"ra": lax.rem(me + 1, n)},
            device_id_type=pl.DeviceIdType.MESH,
        )
        both.wait()

    send_gains(0, 0)

    names = iota((PART, base), 0)
    hot_cols[...] = jnp.zeros_like(hot_cols)
    hot_cols[:, 0:base] = jnp.where(names == pair_ref[0:1, :], 1.0, 0.0)
    hot_cols[:, rows : rows + base] = jnp.where(names == pair_ref[1:2, :], 1.0, 0.0)
    hot_rows[...] = hot_cols[...].T
    key = target_ref[...] * windows + lax.rem(iota((1, held), 1), windows)
    key_hot = jnp.where(iota((n * windows, held), 0) == key, 1.0, 0.0)
    gap = iota((held, lanes), 1) - iota((held, lanes), 0)
    spread = gap == 0
    for b in range(1, GROUP):
        spread = spread | (gap == b * held)
    spread = jnp.where(spread, 1.0, 0.0)
    offset = iota((GROUP, lanes), 1) - held * iota((GROUP, lanes), 0)
    own_lanes = (offset >= 0) & (offset < held)

    raw[pl.ds(base, rows - base)] = jnp.zeros((rows - base, held, width), BF16)

    def turn(k, carry):
        block = raw[pl.ds(k * GROUP, GROUP)].reshape(lanes, width)
        turned[k] = block.T.astype(F32)
        return carry

    for k, copy in enumerate(loads):
        copy.wait()
        lax.fori_loop(k * PIECE // GROUP, min((k + 1) * PIECE, rows) // GROUP, turn, 0)

    flux = None
    for it in range(ITERS):
        finish(2 * it, tables.at[it])
        table = tables[it].reshape(n * windows, LANES)
        chosen = dot(table, key_hot, 0, 0)
        if it == 0:
            flux = chosen[2 * PART : 2 * PART + 1]
        gain_re = dot(hot_rows[...], chosen[0:PART])
        gain_im = dot(hot_rows[...], chosen[PART : 2 * PART])
        g1r, g2r = gain_re[0:rows], gain_re[rows:]
        g1i, g2i = gain_im[0:rows], gain_im[rows:]
        pred[0:rows] = dot(flux * (g1r * g2r + g1i * g2i), spread)
        pred[rows:] = dot(flux * (g1i * g2r - g1r * g2i), spread)

        def work(k, carry):
            low = pl.multiple_of(k * GROUP, GROUP)
            p_re = jnp.sum(
                jnp.where(own_lanes, pred[pl.ds(low, GROUP)], 0.0), axis=0, keepdims=True
            )
            p_im = jnp.sum(
                jnp.where(own_lanes, pred[pl.ds(rows + low, GROUP)], 0.0), axis=0, keepdims=True
            )
            total = [jnp.zeros((8, lanes), F32) for _ in range(3)]
            for c in range(0, half, 8):
                re = turned[k, c : c + 8]
                im = turned[k, half + c : half + c + 8]
                d_re = re - p_re
                d_im = im - p_im
                weight = 1.0 / (d_re * d_re + d_im * d_im + ROBUST)
                total[0] = total[0] + weight
                total[1] = total[1] + weight * re
                total[2] = total[2] + weight * im
            for q in range(3):
                row = jnp.sum(total[q], axis=0, keepdims=True)
                sums[pl.ds(q * rows + low, GROUP)] = jnp.where(own_lanes, row, 0.0)
            return carry

        lax.fori_loop(0, chunks, work, 0)

        total = dot(sums[...], spread, 1, 1)
        w, wr, wi = total[0:rows], total[rows : 2 * rows], total[2 * rows :]
        scale = flux * ROBUST
        square = flux * scale
        terms = (
            (scale * (g2r * wr - g2i * wi), scale * (g1r * wr + g1i * wi)),
            (scale * (g2r * wi + g2i * wr), scale * (g1i * wr - g1r * wi)),
            (square * (g2r * g2r + g2i * g2i) * w, square * (g1r * g1r + g1i * g1i) * w),
        )
        normal = [dot(hot_cols[...], jnp.concatenate(pair, axis=0)) for pair in terms]
        normal.append(normal[2])
        slab = dot(key_hot, jnp.concatenate(normal, axis=0), 1, 1)
        slabs[it] = slab.reshape(n, windows, LANES)
        send_slabs(2 * it + 1, it)
        current = mine[it]
        near = tables[it, lax.rem(me + n - 1, n)] + tables[it, lax.rem(me + 1, n)]
        finish(2 * it + 1, partials.at[it])
        gathered = jnp.sum(partials[it], axis=0)
        denom = pltpu.roll(gathered, 2 * PART, 1)
        own = (gathered + DAMPING * current) / (denom + DAMPING)
        fresh = (1.0 - 2.0 * COUPLING) * own + COUPLING * near
        if it + 1 < ITERS:
            mine[it + 1] = jnp.where(iota(fresh.shape, 1) < 2 * PART, fresh, 0.0)
            send_gains(2 * it + 2, it + 1)
        else:
            out_ref[0, 0] = fresh[:, 0:antennas]
            out_ref[0, 1] = fresh[:, PART : PART + antennas]


def body(
    observed_correlations,
    direction_per_batch,
    receiver_pairings,
    predicted_source_brightness,
    starter_complex_factors,
):
    held, base, width = observed_correlations.shape
    antennas, windows = starter_complex_factors.shape[2:]
    n = lax.axis_size("ra")
    rows = -(-base // PIECE) * PIECE
    lanes = GROUP * held
    pieces = rows // PIECE
    vmem = pl.BlockSpec(memory_space=pltpu.VMEM)
    result = pl.pallas_call(
        functools.partial(kernel, n),
        out_shape=jax.ShapeDtypeStruct((1, 2, windows, antennas), F32),
        in_specs=[pl.BlockSpec(memory_space=pl.ANY)] + [vmem] * 4,
        out_specs=vmem,
        scratch_shapes=[
            pltpu.VMEM((rows, held, width), BF16),
            pltpu.VMEM((rows // GROUP, width, lanes), F32),
            pltpu.VMEM((ITERS, n, windows, LANES), F32),
            pltpu.VMEM((ITERS, windows, LANES), F32),
            pltpu.VMEM((ITERS, n, windows, LANES), F32),
            pltpu.VMEM((ITERS, n, windows, LANES), F32),
            pltpu.VMEM((2 * rows, lanes), F32),
            pltpu.VMEM((3 * rows, lanes), F32),
            pltpu.VMEM((2 * rows, PART), F32),
            pltpu.VMEM((PART, 2 * rows), F32),
            pltpu.SemaphoreType.DMA((pieces,)),
            pltpu.SemaphoreType.DMA((2 * ITERS,)),
            pltpu.SemaphoreType.DMA((2 * ITERS,)),
        ],
        compiler_params=pltpu.CompilerParams(
            collective_id=0, has_side_effects=True, vmem_limit_bytes=56 * 1024 * 1024
        ),
        cost_estimate=pl.CostEstimate(
            flops=60 * held * base * width, bytes_accessed=2 * held * base * width, transcendentals=0
        ),
    )(
        jnp.transpose(observed_correlations, (1, 0, 2)),
        direction_per_batch.T,
        receiver_pairings.T,
        predicted_source_brightness,
        jnp.transpose(starter_complex_factors, (0, 1, 3, 2)),
    )
    return jnp.transpose(result, (0, 1, 3, 2))


def solution(mesh):
    placed = (
        P(("grp", "ra"), None, None),
        P(("grp", "ra"), None),
        P("grp", None),
        P(("grp", "ra"), None),
        P(("grp", "ra"), None, None, None),
    )
    return jax.shard_map(
        body,
        mesh=mesh,
        in_specs=placed,
        out_specs=P(("grp", "ra"), None, None, None),
        check_vma=False,
    )
```

time: 354 us -> 45.1 us (0.13)
  waiting for transfers between devices: 148 us -> 0 us
  other arithmetic: 86.6 us -> 0 us
  starting transfers between devices: 54.2 us -> 0 us
  local copies, waits for them, and re-layouts: 51.9 us -> 1.32 us
  Pallas kernels: 0 us -> 43.4 us
  matrix products: 11.7 us -> 0 us
    all_to_all x2 -> x0, waiting for transfers between devices: 148 us -> none  [the longest x1 148 us: body(): lax.all_to_all(outgoing, 'ra', split_axis=0, concat_axis=0, tiled=True)]
    reduce_sum x8 -> x0, other arithmetic: 62.6 us -> none  [the longest x6 61.6 us: channel_sums(): jnp.sum(weight * data_im, axis=-1)]
    pallas_call x0 -> x1, Pallas kernels: none -> 43.4 us  [body(): pl.pallas_call(functools.partial(kernel, n), out_shape=jax.ShapeDtypeStru...]
    ppermute x4 -> x0, starting transfers between devices: 40.7 us -> none  [the longest x2 39.4 us: with_halo(): lax.ppermute(head, axis, [((i + 1) % count, i) for i in range(count)])]
    gather x2 -> x0, local copies, waits for them, and re-layouts: 40.6 us -> none  [the longest x1 39.3 us: body(): observed_correlations[source_row]]
    convert_element_type x6 -> x0, other arithmetic: 14.9 us -> none  [channel_sums(): data = blocks_data.astype(jnp.float32)]
    all_to_all x2 -> x0, starting transfers between devices: 13.6 us -> none  [the longest x1 7.39 us: body(): lax.all_to_all(labels, 'ra', split_axis=0, concat_axis=0, tiled=True)]
    dot_general x35 -> x0, matrix products: 11.7 us -> none  [the longest x6 2.42 us: antenna_normals(): jnp.dot(one_second, second_receiver_indicator, precision=PRECISE)]
  transfers between devices with their start and end apart: 6 -> 0, of which waited for: 1 -> 0; matrix products, arithmetic and copies ran while one was open for 41% -> 0% of each run, Pallas kernels for 0% -> 0%
where the time goes in v1:
time: 45.1 us; the launch traced here: 44.7 us
  Pallas kernels  43.4 us (96%)
  local copies, waits for them, and re-layouts  1.32 us (3%)
    pallas_call x1, Pallas kernels, body(): pl.pallas_call(functools.partial(kernel, n), out_shape=jax.ShapeDtypeStru...  43.4 us
    unnamed x1, local copies, waits for them, and re-layouts  1.32 us

profile of v1, /device:TPU:0, one launch (start us, length us, event | category | flops | bytes accessed | tf_op | source)
XLA Modules:
  0.0 44.7 jit_solution(5727294757990713022)
XLA Ops:
  0.0 43.4 %shard_map.55 = f32[1,2,16,27]{3,2,1,0:T(8,128)} custom-call(bf16[351,48,128]{2,1,0:T(8,128)(2,1)} %bitcast.5, s32[1,48]{1,0:T(1,128)} %bitcast.9, s32[2,351]{1,0:T(2,128)} %bitcast.8, f32[1,16]{1,0:T(1,128)} %flux_ref.1, f32[1,2,16,27]{3,2,1,0:T(8,128)} %bitcast.7), custom_call_target="tpu_custom_call" | custom-call | flops 129392640 | bytes 4313088 | tf_op jit(solution)/shard_map/pallas_call | solution.py:244
  43.4 1.3 %copy.7 = f32[1,2,27,16]{2,3,1,0:T(8,128)} copy(f32[1,2,27,16]{2,3,1,0:T(8,128)} %bitcast.6) | data formatting | bytes 6912

commit v2 on v1

--- a/solution.py
+++ b/solution.py
@@ -11,7 +11,6 @@
 ROBUST = 0.5
 COUPLING = 0.2
 DAMPING = 100.0
-PRECISE = lax.Precision.HIGHEST
 F32 = jnp.float32
 BF16 = jnp.bfloat16
 
@@ -22,9 +21,12 @@
 
 
 def dot(a, b, ca=1, cb=0):
-    return lax.dot_general(
-        a, b, (((ca,), (cb,)), ((), ())), precision=PRECISE, preferred_element_type=F32
-    )
+    return lax.dot_general(a, b, (((ca,), (cb,)), ((), ())), preferred_element_type=F32)
+
+
+def halves(x):
+    high = x.astype(BF16)
+    return high, (x - high.astype(F32)).astype(BF16)
 
 
 def iota(shape, dim):
@@ -42,13 +44,16 @@
     raw,
     turned,
     tables,
-    mine,
+    message,
     slabs,
     partials,
+    state,
     pred,
     sums,
-    hot_rows,
     hot_cols,
+    to_gains,
+    to_normals,
+    key_hot,
     x_sem,
     send_sem,
     recv_sem,
@@ -56,7 +61,9 @@
     base, held, width = x_ref.shape
     rows = raw.shape[0]
     chunks = rows // GROUP
+    places = sums.shape[1]
     lanes = GROUP * held
+    span = hot_cols.shape[1] // 2
     half = width // 2
     antennas = start_ref.shape[3]
     windows = start_ref.shape[2]
@@ -84,12 +91,60 @@
 
     lax.fori_loop(1, n, greet, 0)
 
+    lane = iota((windows, LANES), 1)
+
+    def pack(x):
+        once = pltpu.roll(x, PART, 1)
+        twice = pltpu.roll(x, 2 * PART, 1)
+        wide = jnp.where(lane < PART, x, jnp.where(lane < 3 * PART, once, twice))
+        high = wide.astype(BF16).astype(F32)
+        is_high = (lane < PART) | ((lane >= 2 * PART) & (lane < 3 * PART))
+        return jnp.where(is_high, high, wide - high).astype(BF16)
+
+    def unpack(x):
+        x = x + pltpu.roll(x, LANES - PART, 1)
+        return jnp.where(lane < PART, x, pltpu.roll(x, LANES - PART, 1))
+
     eye = iota((windows, windows), 0) == iota((windows, windows), 1)
     flux_col = jnp.sum(jnp.where(eye, flux_ref[...], 0.0), axis=1, keepdims=True)
-    mine[...] = jnp.zeros_like(mine)
-    mine[0, :, 0:antennas] = start_ref[0, 0]
-    mine[0, :, PART : PART + antennas] = start_ref[0, 1]
-    mine[0, :, 2 * PART : 2 * PART + 1] = flux_col
+    state[...] = jnp.zeros_like(state)
+    state[:, 0:antennas] = start_ref[0, 0]
+    state[:, antennas : antennas + 1] = flux_col
+    state[:, PART : PART + antennas] = start_ref[0, 1]
+    current = state[...]
+    message[0] = pack(current)
+
+    names = iota((PART, base), 0)
+    hot_cols[...] = jnp.zeros_like(hot_cols)
+    hot_cols[:, 0:base] = jnp.where(names == pair_ref[0:1, :], 1.0, 0.0)
+    hot_cols[:, span : span + base] = jnp.where(names == pair_ref[1:2, :], 1.0, 0.0)
+    position = iota((1, GROUP * places), 1)
+    part = jnp.zeros_like(position)
+    for b in range(1, GROUP):
+        part = part + jnp.where(position >= b * places, 1, 0)
+    wanted = (position - places * part) * GROUP + part
+    order = jnp.where(iota((span, GROUP * places), 0) == wanted, 1.0, 0.0).astype(BF16)
+    hot_first = dot(hot_cols[:, 0:span].astype(BF16), order)
+    hot_second = dot(hot_cols[:, span:].astype(BF16), order)
+    for s, hot in enumerate((hot_first, hot_second)):
+        twice = jnp.concatenate([hot, hot], axis=0).T
+        to_gains[s * GROUP * places : (s + 1) * GROUP * places] = twice.astype(BF16)
+    for b in range(GROUP):
+        cut = slice(b * places, (b + 1) * places)
+        pieces = [hot_first[:, cut]] * 2 + [hot_second[:, cut]] * 2
+        to_normals[b * PART : (b + 1) * PART] = jnp.concatenate(pieces, axis=1).astype(BF16)
+    key = target_ref[...] * windows + lax.rem(iota((1, held), 1), windows)
+    keys = jnp.concatenate([key] * GROUP, axis=1)
+    key_hot[...] = jnp.where(iota((n * windows, lanes), 0) == keys, 1.0, 0.0).astype(BF16)
+    column = iota((1, lanes), 1)
+    own_lanes = [(column >= b * held) & (column < (b + 1) * held) for b in range(GROUP)]
+
+    def fold(x):
+        size = x.shape[0] // GROUP
+        out = x[0:size]
+        for b in range(1, GROUP):
+            out = jnp.where(own_lanes[b], x[b * size : (b + 1) * size], out)
+        return out
 
     pl.semaphore_wait(barrier, n - 1)
 
@@ -105,11 +160,11 @@
 
     def send_gains(phase, it):
         def step(k, carry):
-            copy_to(phase, mine.at[it], tables.at[it], k).start()
+            copy_to(phase, message.at[it], tables.at[it], k).start()
             return carry
 
         lax.fori_loop(1, n, step, 0)
-        tables[it, me] = mine[it]
+        tables[it, me] = message[it]
 
     def send_slabs(phase, it):
         def step(k, carry):
@@ -133,22 +188,9 @@
 
     send_gains(0, 0)
 
-    names = iota((PART, base), 0)
-    hot_cols[...] = jnp.zeros_like(hot_cols)
-    hot_cols[:, 0:base] = jnp.where(names == pair_ref[0:1, :], 1.0, 0.0)
-    hot_cols[:, rows : rows + base] = jnp.where(names == pair_ref[1:2, :], 1.0, 0.0)
-    hot_rows[...] = hot_cols[...].T
-    key = target_ref[...] * windows + lax.rem(iota((1, held), 1), windows)
-    key_hot = jnp.where(iota((n * windows, held), 0) == key, 1.0, 0.0)
-    gap = iota((held, lanes), 1) - iota((held, lanes), 0)
-    spread = gap == 0
-    for b in range(1, GROUP):
-        spread = spread | (gap == b * held)
-    spread = jnp.where(spread, 1.0, 0.0)
-    offset = iota((GROUP, lanes), 1) - held * iota((GROUP, lanes), 0)
-    own_lanes = (offset >= 0) & (offset < held)
-
     raw[pl.ds(base, rows - base)] = jnp.zeros((rows - base, held, width), BF16)
+    for q in range(3):
+        sums[q] = jnp.zeros((places, lanes), F32)
 
     def turn(k, carry):
         block = raw[pl.ds(k * GROUP, GROUP)].reshape(lanes, width)
@@ -162,44 +204,37 @@
     flux = None
     for it in range(ITERS):
         finish(2 * it, tables.at[it])
-        table = tables[it].reshape(n * windows, LANES)
-        chosen = dot(table, key_hot, 0, 0)
+        chosen = dot(tables[it].reshape(n * windows, LANES), key_hot[...], 0, 0)
         if it == 0:
-            flux = chosen[2 * PART : 2 * PART + 1]
-        gain_re = dot(hot_rows[...], chosen[0:PART])
-        gain_im = dot(hot_rows[...], chosen[PART : 2 * PART])
-        g1r, g2r = gain_re[0:rows], gain_re[rows:]
-        g1i, g2i = gain_im[0:rows], gain_im[rows:]
-        pred[0:rows] = dot(flux * (g1r * g2r + g1i * g2i), spread)
-        pred[rows:] = dot(flux * (g1i * g2r - g1r * g2i), spread)
+            flux = chosen[antennas : antennas + 1] + chosen[PART + antennas : PART + antennas + 1]
+        gain_re = dot(to_gains[...], chosen[0 : 2 * PART].astype(BF16))
+        gain_im = dot(to_gains[...], chosen[2 * PART :].astype(BF16))
+        side = GROUP * places
+        g1r, g2r = fold(gain_re[0:side]), fold(gain_re[side:])
+        g1i, g2i = fold(gain_im[0:side]), fold(gain_im[side:])
+        pred[0] = flux * (g1r * g2r + g1i * g2i)
+        pred[1] = flux * (g1i * g2r - g1r * g2i)
 
         def work(k, carry):
-            low = pl.multiple_of(k * GROUP, GROUP)
-            p_re = jnp.sum(
-                jnp.where(own_lanes, pred[pl.ds(low, GROUP)], 0.0), axis=0, keepdims=True
-            )
-            p_im = jnp.sum(
-                jnp.where(own_lanes, pred[pl.ds(rows + low, GROUP)], 0.0), axis=0, keepdims=True
-            )
+            p_re = pred[0, pl.ds(k, 1)]
+            p_im = pred[1, pl.ds(k, 1)]
             total = [jnp.zeros((8, lanes), F32) for _ in range(3)]
             for c in range(0, half, 8):
                 re = turned[k, c : c + 8]
                 im = turned[k, half + c : half + c + 8]
                 d_re = re - p_re
                 d_im = im - p_im
-                weight = 1.0 / (d_re * d_re + d_im * d_im + ROBUST)
+                weight = pl.reciprocal(d_re * d_re + d_im * d_im + ROBUST, approx=True)
                 total[0] = total[0] + weight
                 total[1] = total[1] + weight * re
                 total[2] = total[2] + weight * im
             for q in range(3):
-                row = jnp.sum(total[q], axis=0, keepdims=True)
-                sums[pl.ds(q * rows + low, GROUP)] = jnp.where(own_lanes, row, 0.0)
+                sums[q, pl.ds(k, 1)] = jnp.sum(total[q], axis=0, keepdims=True)
             return carry
 
         lax.fori_loop(0, chunks, work, 0)
 
-        total = dot(sums[...], spread, 1, 1)
-        w, wr, wi = total[0:rows], total[rows : 2 * rows], total[2 * rows :]
+        w, wr, wi = sums[0], sums[1], sums[2]
         scale = flux * ROBUST
         square = flux * scale
         terms = (
@@ -207,20 +242,26 @@
             (scale * (g2r * wi + g2i * wr), scale * (g1i * wr - g1r * wi)),
             (square * (g2r * g2r + g2i * g2i) * w, square * (g1r * g1r + g1i * g1i) * w),
         )
-        normal = [dot(hot_cols[...], jnp.concatenate(pair, axis=0)) for pair in terms]
+        normal = []
+        for one_first, one_second in terms:
+            parts = jnp.concatenate(halves(one_first) + halves(one_second), axis=0)
+            normal.append(fold(dot(to_normals[...], parts)))
         normal.append(normal[2])
-        slab = dot(key_hot, jnp.concatenate(normal, axis=0), 1, 1)
+        high, low = halves(jnp.concatenate(normal, axis=0))
+        slab = dot(key_hot[...], high, 1, 1) + dot(key_hot[...], low, 1, 1)
         slabs[it] = slab.reshape(n, windows, LANES)
         send_slabs(2 * it + 1, it)
-        current = mine[it]
-        near = tables[it, lax.rem(me + n - 1, n)] + tables[it, lax.rem(me + 1, n)]
+        before = tables[it, lax.rem(me + n - 1, n)].astype(F32)
+        after = tables[it, lax.rem(me + 1, n)].astype(F32)
+        near = unpack(before + after)
         finish(2 * it + 1, partials.at[it])
         gathered = jnp.sum(partials[it], axis=0)
         denom = pltpu.roll(gathered, 2 * PART, 1)
         own = (gathered + DAMPING * current) / (denom + DAMPING)
         fresh = (1.0 - 2.0 * COUPLING) * own + COUPLING * near
         if it + 1 < ITERS:
-            mine[it + 1] = jnp.where(iota(fresh.shape, 1) < 2 * PART, fresh, 0.0)
+            current = jnp.where(lane < 2 * PART, fresh, 0.0)
+            message[it + 1] = pack(current)
             send_gains(2 * it + 2, it + 1)
         else:
             out_ref[0, 0] = fresh[:, 0:antennas]
@@ -240,6 +281,8 @@
     rows = -(-base // PIECE) * PIECE
     lanes = GROUP * held
     pieces = rows // PIECE
+    places = -(-(rows // GROUP) // 16) * 16
+    span = -(-rows // LANES) * LANES
     vmem = pl.BlockSpec(memory_space=pltpu.VMEM)
     result = pl.pallas_call(
         functools.partial(kernel, n),
@@ -249,14 +292,17 @@
         scratch_shapes=[
             pltpu.VMEM((rows, held, width), BF16),
             pltpu.VMEM((rows // GROUP, width, lanes), F32),
-            pltpu.VMEM((ITERS, n, windows, LANES), F32),
-            pltpu.VMEM((ITERS, windows, LANES), F32),
+            pltpu.VMEM((ITERS, n, windows, LANES), BF16),
+            pltpu.VMEM((ITERS, windows, LANES), BF16),
             pltpu.VMEM((ITERS, n, windows, LANES), F32),
             pltpu.VMEM((ITERS, n, windows, LANES), F32),
-            pltpu.VMEM((2 * rows, lanes), F32),
-            pltpu.VMEM((3 * rows, lanes), F32),
-            pltpu.VMEM((2 * rows, PART), F32),
-            pltpu.VMEM((PART, 2 * rows), F32),
+            pltpu.VMEM((windows, LANES), F32),
+            pltpu.VMEM((2, places, lanes), F32),
+            pltpu.VMEM((3, places, lanes), F32),
+            pltpu.VMEM((PART, 2 * span), F32),
+            pltpu.VMEM((2 * GROUP * places, 2 * PART), BF16),
+            pltpu.VMEM((GROUP * PART, 4 * places), BF16),
+            pltpu.VMEM((n * windows, lanes), BF16),
             pltpu.SemaphoreType.DMA((pieces,)),
             pltpu.SemaphoreType.DMA((2 * ITERS,)),
             pltpu.SemaphoreType.DMA((2 * ITERS,)),

time: 45.1 us -> 34.3 us (0.76)
  Pallas kernels: 43.4 us -> 32.6 us
    pallas_call x1, Pallas kernels: 43.4 us -> 32.6 us  [body(): pl.pallas_call(functools.partial(kernel, n), out_shape=jax.ShapeDtypeStru...]
where the time goes in v2:
time: 34.3 us; the launch traced here: 33.9 us
  Pallas kernels  32.6 us (95%)
  local copies, waits for them, and re-layouts  1.32 us (4%)
    pallas_call x1, Pallas kernels, body(): pl.pallas_call(functools.partial(kernel, n), out_shape=jax.ShapeDtypeStru...  32.6 us
    unnamed x1, local copies, waits for them, and re-layouts  1.32 us

profile of v2, /device:TPU:0, one launch (start us, length us, event | category | flops | bytes accessed | tf_op | source)
XLA Modules:
  0.0 33.9 jit_solution(3603199244660169900)
XLA Ops:
  0.0 32.6 %shard_map.55 = f32[1,2,16,27]{3,2,1,0:T(8,128)} custom-call(bf16[351,48,128]{2,1,0:T(8,128)(2,1)} %bitcast.5, s32[1,48]{1,0:T(1,128)} %bitcast.9, s32[2,351]{1,0:T(2,128)} %bitcast.8, f32[1,16]{1,0:T(1,128)} %flux_ref.1, f32[1,2,16,27]{3,2,1,0:T(8,128)} %bitcast.7), custom_call_target="tpu_custom_call" | custom-call | flops 129392640 | bytes 4313088 | tf_op jit(solution)/shard_map/pallas_call | solution.py:287
  32.6 1.3 %copy.7 = f32[1,2,27,16]{2,3,1,0:T(8,128)} copy(f32[1,2,27,16]{2,3,1,0:T(8,128)} %bitcast.6) | data formatting | bytes 6912

commit v3 on v2

--- a/solution.py
+++ b/solution.py
@@ -18,6 +18,7 @@
 PART = 32
 LANES = 128
 PIECE = 32
+UNROLL = 4
 
 
 def dot(a, b, ca=1, cb=0):
@@ -67,6 +68,8 @@
     half = width // 2
     antennas = start_ref.shape[3]
     windows = start_ref.shape[2]
+    kept = windows * 3 * PART // LANES
+    rest = windows - kept
     me = lax.axis_index("ra")
 
     loads = []
@@ -148,10 +151,10 @@
 
     pl.semaphore_wait(barrier, n - 1)
 
-    def copy_to(phase, source, place, k):
+    def copy_to(phase, source, target, k):
         return pltpu.make_async_remote_copy(
             src_ref=source,
-            dst_ref=place.at[me],
+            dst_ref=target,
             send_sem=send_sem.at[phase],
             recv_sem=recv_sem.at[phase],
             device_id={"ra": lax.rem(me + k, n)},
@@ -160,7 +163,7 @@
 
     def send_gains(phase, it):
         def step(k, carry):
-            copy_to(phase, message.at[it], tables.at[it], k).start()
+            copy_to(phase, message.at[it], tables.at[it, me], k).start()
             return carry
 
         lax.fori_loop(1, n, step, 0)
@@ -168,14 +171,14 @@
 
     def send_slabs(phase, it):
         def step(k, carry):
-            copy_to(phase, slabs.at[it, lax.rem(me + k, n)], partials.at[it], k).start()
+            source = slabs.at[it, lax.rem(me + k, n), pl.ds(0, kept)]
+            copy_to(phase, source, partials.at[it, me, pl.ds(0, kept)], k).start()
             return carry
 
         lax.fori_loop(1, n, step, 0)
-        partials[it, me] = slabs[it, me]
-
-    def finish(phase, place):
-        whole = place.at[pl.ds(0, n - 1)]
+        partials[it, me, 0:kept] = slabs[it, me, 0:kept]
+
+    def finish(phase, whole):
         both = pltpu.make_async_remote_copy(
             src_ref=whole,
             dst_ref=whole,
@@ -203,7 +206,7 @@
 
     flux = None
     for it in range(ITERS):
-        finish(2 * it, tables.at[it])
+        finish(2 * it, tables.at[it, pl.ds(0, n - 1)])
         chosen = dot(tables[it].reshape(n * windows, LANES), key_hot[...], 0, 0)
         if it == 0:
             flux = chosen[antennas : antennas + 1] + chosen[PART + antennas : PART + antennas + 1]
@@ -232,7 +235,7 @@
                 sums[q, pl.ds(k, 1)] = jnp.sum(total[q], axis=0, keepdims=True)
             return carry
 
-        lax.fori_loop(0, chunks, work, 0)
+        lax.fori_loop(0, chunks, work, 0, unroll=UNROLL)
 
         w, wr, wi = sums[0], sums[1], sums[2]
         scale = flux * ROBUST
@@ -246,17 +249,32 @@
         for one_first, one_second in terms:
             parts = jnp.concatenate(halves(one_first) + halves(one_second), axis=0)
             normal.append(fold(dot(to_normals[...], parts)))
-        normal.append(normal[2])
+        normal.append(jnp.zeros_like(normal[2]))
         high, low = halves(jnp.concatenate(normal, axis=0))
         slab = dot(key_hot[...], high, 1, 1) + dot(key_hot[...], low, 1, 1)
-        slabs[it] = slab.reshape(n, windows, LANES)
+        slab = slab.reshape(n, windows, LANES)
+        last = slab[:, kept:]
+        fill = [pltpu.roll(last, LANES - (q + 1) * PART, 2) for q in range(3)]
+        fill = jnp.concatenate(fill, axis=1)
+        slabs[it, :, 0:kept] = jnp.where(
+            iota((n, kept, LANES), 2) < 3 * PART, slab[:, 0:kept], fill
+        )
         send_slabs(2 * it + 1, it)
         before = tables[it, lax.rem(me + n - 1, n)].astype(F32)
         after = tables[it, lax.rem(me + 1, n)].astype(F32)
         near = unpack(before + after)
-        finish(2 * it + 1, partials.at[it])
-        gathered = jnp.sum(partials[it], axis=0)
-        denom = pltpu.roll(gathered, 2 * PART, 1)
+        finish(2 * it + 1, partials.at[it, pl.ds(0, n - 1), pl.ds(0, kept)])
+        gathered = jnp.sum(partials[it, :, 0:kept], axis=0)
+        last = jnp.zeros((rest, LANES), F32)
+        for q in range(3):
+            moved = pltpu.roll(gathered[q * rest : (q + 1) * rest], (q + 1) * PART, 1)
+            last = jnp.where(lane[0:rest] // PART == q, moved, last)
+        gathered = jnp.concatenate([gathered, last], axis=0)
+        denom = jnp.where(
+            lane < PART,
+            pltpu.roll(gathered, 2 * PART, 1),
+            pltpu.roll(gathered, 3 * PART, 1),
+        )
         own = (gathered + DAMPING * current) / (denom + DAMPING)
         fresh = (1.0 - 2.0 * COUPLING) * own + COUPLING * near
         if it + 1 < ITERS:

time: 34.3 us -> 33.5 us (0.977)
  Pallas kernels: 32.6 us -> 31.8 us
    pallas_call x1, Pallas kernels: 32.6 us -> 31.8 us  [body(): pl.pallas_call(functools.partial(kernel, n), out_shape=jax.ShapeDtypeStru...]
where the time goes in v3:
time: 33.5 us; the launch traced here: 33.1 us
  Pallas kernels  31.8 us (95%)
  local copies, waits for them, and re-layouts  1.32 us (4%)
    pallas_call x1, Pallas kernels, body(): pl.pallas_call(functools.partial(kernel, n), out_shape=jax.ShapeDtypeStru...  31.8 us
    unnamed x1, local copies, waits for them, and re-layouts  1.32 us

profile of v3, /device:TPU:0, one launch (start us, length us, event | category | flops | bytes accessed | tf_op | source)
XLA Modules:
  0.0 33.1 jit_solution(11105801308758403725)
XLA Ops:
  0.0 31.8 %shard_map.55 = f32[1,2,16,27]{3,2,1,0:T(8,128)} custom-call(bf16[351,48,128]{2,1,0:T(8,128)(2,1)} %bitcast.5, s32[1,48]{1,0:T(1,128)} %bitcast.9, s32[2,351]{1,0:T(2,128)} %bitcast.8, f32[1,16]{1,0:T(1,128)} %flux_ref.1, f32[1,2,16,27]{3,2,1,0:T(8,128)} %bitcast.7), custom_call_target="tpu_custom_call" | custom-call | flops 129392640 | bytes 4313088 | tf_op jit(solution)/shard_map/pallas_call | solution.py:305
  31.8 1.3 %copy.7 = f32[1,2,27,16]{2,3,1,0:T(8,128)} copy(f32[1,2,27,16]{2,3,1,0:T(8,128)} %bitcast.6) | data formatting | bytes 6912

commit v4 on v3

--- a/solution.py
+++ b/solution.py
@@ -32,6 +32,12 @@
 
 def iota(shape, dim):
     return lax.broadcasted_iota(jnp.int32, shape, dim)
+
+
+def peer(me, n, k):
+    odd = lax.rem(k, 2)
+    away = lax.div(k + 1, 2)
+    return lax.rem(me + odd * away + (1 - odd) * (n - away), n)
 
 
 def kernel(
@@ -87,7 +93,7 @@
         pl.semaphore_signal(
             barrier,
             inc=1,
-            device_id={"ra": lax.rem(me + k, n)},
+            device_id={"ra": peer(me, n, k)},
             device_id_type=pl.DeviceIdType.MESH,
         )
         return carry
@@ -157,7 +163,7 @@
             dst_ref=target,
             send_sem=send_sem.at[phase],
             recv_sem=recv_sem.at[phase],
-            device_id={"ra": lax.rem(me + k, n)},
+            device_id={"ra": peer(me, n, k)},
             device_id_type=pl.DeviceIdType.MESH,
         )
 
@@ -171,15 +177,15 @@
 
     def send_slabs(phase, it):
         def step(k, carry):
-            source = slabs.at[it, lax.rem(me + k, n), pl.ds(0, kept)]
+            source = slabs.at[it, peer(me, n, k), pl.ds(0, kept)]
             copy_to(phase, source, partials.at[it, me, pl.ds(0, kept)], k).start()
             return carry
 
         lax.fori_loop(1, n, step, 0)
         partials[it, me, 0:kept] = slabs[it, me, 0:kept]
 
-    def finish(phase, whole):
-        both = pltpu.make_async_remote_copy(
+    def all_of(phase, whole):
+        return pltpu.make_async_remote_copy(
             src_ref=whole,
             dst_ref=whole,
             send_sem=send_sem.at[phase],
@@ -187,7 +193,6 @@
             device_id={"ra": lax.rem(me + 1, n)},
             device_id_type=pl.DeviceIdType.MESH,
         )
-        both.wait()
 
     send_gains(0, 0)
 
@@ -205,8 +210,10 @@
         lax.fori_loop(k * PIECE // GROUP, min((k + 1) * PIECE, rows) // GROUP, turn, 0)
 
     flux = None
+    sent = []
     for it in range(ITERS):
-        finish(2 * it, tables.at[it, pl.ds(0, n - 1)])
+        gains_done = all_of(2 * it, tables.at[it, pl.ds(0, n - 1)])
+        gains_done.wait_recv()
         chosen = dot(tables[it].reshape(n * windows, LANES), key_hot[...], 0, 0)
         if it == 0:
             flux = chosen[antennas : antennas + 1] + chosen[PART + antennas : PART + antennas + 1]
@@ -263,7 +270,9 @@
         before = tables[it, lax.rem(me + n - 1, n)].astype(F32)
         after = tables[it, lax.rem(me + 1, n)].astype(F32)
         near = unpack(before + after)
-        finish(2 * it + 1, partials.at[it, pl.ds(0, n - 1), pl.ds(0, kept)])
+        slabs_done = all_of(2 * it + 1, partials.at[it, pl.ds(0, n - 1), pl.ds(0, kept)])
+        slabs_done.wait_recv()
+        sent.extend([gains_done, slabs_done])
         gathered = jnp.sum(partials[it, :, 0:kept], axis=0)
         last = jnp.zeros((rest, LANES), F32)
         for q in range(3):
@@ -284,6 +293,8 @@
         else:
             out_ref[0, 0] = fresh[:, 0:antennas]
             out_ref[0, 1] = fresh[:, PART : PART + antennas]
+    for copies in sent:
+        copies.wait_send()
 
 
 def body(

time: 33.5 us -> 33 us (0.985)
  Pallas kernels: 31.8 us -> 31.3 us
    pallas_call x1, Pallas kernels: 31.8 us -> 31.3 us  [body(): pl.pallas_call(functools.partial(kernel, n), out_shape=jax.ShapeDtypeStru...]
where the time goes in v4:
time: 33 us; the launch traced here: 32.7 us
  Pallas kernels  31.3 us (95%)
  local copies, waits for them, and re-layouts  1.32 us (4%)
    pallas_call x1, Pallas kernels, body(): pl.pallas_call(functools.partial(kernel, n), out_shape=jax.ShapeDtypeStru...  31.3 us
    unnamed x1, local copies, waits for them, and re-layouts  1.32 us

profile of v4, /device:TPU:0, one launch (start us, length us, event | category | flops | bytes accessed | tf_op | source)
XLA Modules:
  0.0 32.7 jit_solution(18429943809324268570)
XLA Ops:
  0.0 31.3 %shard_map.55 = f32[1,2,16,27]{3,2,1,0:T(8,128)} custom-call(bf16[351,48,128]{2,1,0:T(8,128)(2,1)} %bitcast.5, s32[1,48]{1,0:T(1,128)} %bitcast.9, s32[2,351]{1,0:T(2,128)} %bitcast.8, f32[1,16]{1,0:T(1,128)} %flux_ref.1, f32[1,2,16,27]{3,2,1,0:T(8,128)} %bitcast.7), custom_call_target="tpu_custom_call" | custom-call | flops 129392640 | bytes 4313088 | tf_op jit(solution)/shard_map/pallas_call | solution.py:316
  31.3 1.3 %copy.7 = f32[1,2,27,16]{2,3,1,0:T(8,128)} copy(f32[1,2,27,16]{2,3,1,0:T(8,128)} %bitcast.6) | data formatting | bytes 6912
